TPU v7x, 32 devices: a whole 2x2x4 slice. The times are simulated.
32 devices in a mesh: rep: 4 (over x, core), shard: 8 (over z, y).
Axes of the slice: x: 2, y: 2, z: 4, core: 2. Of those that a mesh axis runs over, the one named last changes fastest.
Arguments:
- conv_input: bfloat16 [32, 256, 6144], P(('rep', 'shard')), may hold values from -24 to 24
- cotangent: bfloat16 [32, 256, 6144], P(('rep', 'shard')), may hold values from -6 to 6
- kernel: bfloat16 [31, 6144], P(None, 'shard'), may hold values from -1 to 1
- conv_bias: bfloat16 [6144], P('shard'), may hold values from -3 to 3
- ln_gain: bfloat16 [6144], P('shard'), may hold values from 0.25 to 1.75
- ln_bias: bfloat16 [6144], P('shard'), may hold values from -3 to 3
Outputs:
- activated: bfloat16 [32, 256, 6144], P(('rep', 'shard'))
- grad_input: bfloat16 [32, 256, 6144], P(('rep', 'shard'))
- grad_kernel: float32 [31, 6144], P(None, 'shard')
- grad_conv_bias: float32 [6144], P('shard')
- grad_gain: float32 [6144], P('shard')
- grad_ln_bias: float32 [6144], P('shard')
All inputs are finite; a program needn't handle non-finite values.
Results may differ from a plain program's by a relative error of at most 0.0012.
Values may be sent and summed in bfloat16 or wider, within the bound.
A program may use at most 128 MiB of HBM per device.

v0:
```python
import math

import jax
import jax.numpy as jnp
from jax import lax
from jax.sharding import PartitionSpec as P


def forward_part(frames_in, params):
    taps = params.shape[0] - 3
    half_width = (taps - 1) // 2
    length = frames_in.shape[0]
    padded = jnp.pad(frames_in, ((half_width, half_width), (0, 0)))
    conv_out = params[taps].astype(jnp.float32)[None, :] + params[0].astype(jnp.float32) * padded[
        0:length
    ].astype(jnp.float32)
    for lag_index in range(1, taps):
        conv_out = conv_out + params[lag_index].astype(jnp.float32) * padded[
            lag_index : lag_index + length
        ].astype(jnp.float32)
    row_mean = jnp.mean(conv_out, axis=-1, keepdims=True)
    centered = conv_out - row_mean
    inverse = lax.rsqrt(jnp.mean(centered * centered, axis=-1, keepdims=True) + 1e-05)
    normed = centered * inverse
    affine = params[taps + 1].astype(jnp.float32) * normed + params[taps + 2].astype(jnp.float32)
    squash = jax.nn.sigmoid(affine)
    activated = (affine * squash).astype(jnp.bfloat16)
    return (activated, normed, inverse, affine, squash)


def backward_part(frames_in, upstream, params, normed, inverse, affine, squash):
    taps = params.shape[0] - 3
    half_width = (taps - 1) // 2
    length = frames_in.shape[0]
    grad_affine = upstream.astype(jnp.float32) * squash * (1.0 + affine * (1.0 - squash))
    grad_normed = grad_affine * params[taps + 1].astype(jnp.float32)
    grad_conv = inverse * (
        grad_normed
        - jnp.mean(grad_normed, axis=-1, keepdims=True)
        - normed * jnp.mean(grad_normed * normed, axis=-1, keepdims=True)
    )
    padded_in = jnp.pad(frames_in, ((half_width, half_width), (0, 0)))
    kernel_rows = [
        jnp.sum(grad_conv * padded_in[lag_index : lag_index + length].astype(jnp.float32), axis=0)
        for lag_index in range(taps)
    ]
    padded_grad = jnp.pad(grad_conv, ((half_width, half_width), (0, 0)))
    back_start = 2 * half_width
    grad_input = params[0].astype(jnp.float32) * padded_grad[back_start : back_start + length]
    for lag_index in range(1, taps):
        first = back_start - lag_index
        grad_input = (
            grad_input + params[lag_index].astype(jnp.float32) * padded_grad[first : first + length]
        )
    terms = jnp.concatenate(
        [
            jnp.stack(kernel_rows, 0),
            jnp.sum(grad_conv, axis=0)[None],
            jnp.sum(grad_affine * normed, axis=0)[None],
            jnp.sum(grad_affine, axis=0)[None],
        ],
        0,
    )
    return (grad_input.astype(jnp.bfloat16), terms)


def per_device(conv_input, cotangent, kernel, conv_bias, ln_gain, ln_bias):
    taps = kernel.shape[0]
    packed = jnp.concatenate([kernel, conv_bias[None], ln_gain[None], ln_bias[None]], 0)
    gathered = lax.all_gather(packed, "shard", axis=1, tiled=True)
    activated, normed, inverse, affine, squash = jax.vmap(forward_part, in_axes=(0, None))(
        conv_input, gathered
    )
    again = lax.all_gather(packed, "shard", axis=1, tiled=True)
    grad_input, terms = jax.vmap(backward_part, in_axes=(0, 0, None, 0, 0, 0, 0))(
        conv_input, cotangent, again, normed, inverse, affine, squash
    )
    terms = jnp.sum(terms, axis=0)
    replicas = lax.axis_size("rep")
    groups = lax.axis_size("shard")
    share_sum = lax.psum_scatter(terms, "shard", scatter_dimension=1, tiled=True)
    summed = lax.psum(share_sum, "rep")
    factor = 1.0 / math.sqrt(conv_input.shape[0] * conv_input.shape[1] * replicas * groups)
    grads = summed * factor
    return (activated, grad_input, grads[:taps], grads[taps], grads[taps + 1], grads[taps + 2])


def solution(mesh):
    in_specs = (
        P(("rep", "shard"), None, None),
        P(("rep", "shard"), None, None),
        P(None, "shard"),
        P("shard"),
        P("shard"),
        P("shard"),
    )
    out_specs = (
        P(("rep", "shard"), None, None),
        P(("rep", "shard"), None, None),
        P(None, "shard"),
        P("shard"),
        P("shard"),
        P("shard"),
    )
    return jax.shard_map(
        per_device, mesh=mesh, in_specs=in_specs, out_specs=out_specs, check_vma=False
    )
```

profile of v0, /device:TPU:13, one launch (start us, length us, event | category | flops | bytes accessed | tf_op | source)
XLA Modules:
  0.0 325.0 jit_solution(17576932753638523696)
XLA Ops:
  7.2 0.0 reduce-scatter.2.cloned.1.call-start
  7.2 0.7 broadcast_in_dim.12
  7.9 0.7 broadcast_in_dim.13
  8.6 0.7 broadcast_in_dim.14
  9.3 0.8 pad_maximum_fusion
  10.1 23.0 %all_gather.4 = bf16[34,6144]{1,0:T(8,128)(2,1)S(1)} all-gather(bf16[34,768]{1,0:T(8,128)(2,1)S(1)} %pad_maximum_fusion), channel_id=1, replica_groups=mesh['rep'=4,'shard'=8] {'shard'}, dimensions={1}, use_global_device_ids=true | all-gather | bytes 470016 | tf_op jit(solution)/shard_map/all_gather | solution.py:70
  33.1 0.8 slice_convert_fusion.32
  33.9 1.0 slice_convert_fusion.33
  34.9 75.1 %fusion.123 = (f32[256]{0:T(256)S(1)}, f32[1,256,6144]{2,1,0:T(8,128)}) fusion(f32[6144]{0:T(1024)S(1)} %bitcast.100, f32[6144]{0:T(1024)S(1)} %bitcast.102, f32[6144]{0:T(1024)} %bitcast.104, f32[6144]{0:T(1024)} %bitcast.106, f32[6144]{0:T(1024)} %bitcast.108, f32[6144]{0:T(1024)} %bitcast.110, f32[6144]{0:T(1024)} %bitcast.112, f32[6144]{0:T(1024)} %bitcast.114, ...), kind=kLoop, calls=%fused_computation.269 | loop fusion | flops 147848960 | bytes 10224640 | tf_op jit(solution)/shard_map/vmap()/reduce_sum | solution.py:21
  110.1 0.0 copy-start.1
  110.1 3.7 %multiply_reduce_fusion.2 = f32[256]{0:T(256)S(1)} fusion(f32[1,256,6144]{2,1,0:T(8,128)} %get-tuple-element.48, f32[256]{0:T(256)S(1)} %broadcast_multiply_fusion.3), kind=kLoop, calls=%fused_computation.222 | loop fusion | flops 4718336 | bytes 6293504 | tf_op jit(solution)/shard_map/vmap()/reduce_sum | solution.py:23
  113.8 0.0 copy-done.3
  113.8 0.9 copy-done.1
  114.7 8.9 %multiply_reduce_fusion = (f32[6144]{0:T(1024)}, f32[256]{0:T(256)S(1)}, f32[256]{0:T(256)S(1)}, f32[6144]{0:T(1024)}, f32[1,256,6144]{2,1,0:T(8,128)S(1)}, /*index=5*/bf16[1,256,6144]{2,1,0:T(8,128)(2,1)}) fusion(f32[1,256,6144]{2,1,0:T(8,128)S(1)} %copy-done.1, f32[256]{0:T(256)S(1)} %add_rsqrt_fusion, f32[256]{0:T(256)S(1)} %broadcast_multiply_fusion.3, ...), kind=kLoop, calls=%fused_computation.215 | loop fusion | flops 34590208 | bytes 18976768 | tf_op jit(solution)/shard_map/vmap()/reduce_sum | solution.py:59
  123.6 0.0 copy-done.2
  123.6 0.0 copy-done.19
  123.6 11.0 %fusion.122 = (f32[6144]{0:T(1024)S(1)}, f32[6144]{0:T(1024)S(1)}, f32[6144]{0:T(1024)S(1)}, f32[6144]{0:T(1024)S(1)}, f32[6144]{0:T(1024)S(1)}, /*index=5*/f32[...) fusion(bf16[1,256,6144]{2,1,0:T(8,128)(2,1)S(1)} %copy-done.2, ...), kind=kLoop, calls=%fused_computation.214 | loop fusion | flops 53422080 | bytes 22269952 | tf_op jit(solution)/shard_map/vmap()/reduce_sum | solution.py:44
  134.7 0.0 copy-start
  134.7 3.7 %fusion.89 = (f32[6144]{0:T(1024)S(1)}, f32[6144]{0:T(1024)S(1)}, f32[6144]{0:T(1024)S(1)}, f32[6144]{0:T(1024)S(1)}) fusion(f32[1,256,6144]{2,1,0:T(8,128)S(1)} %get-tuple-element.45, bf16[1,256,6144]{2,1,0:T(8,128)(2,1)S(1)} %copy-done.2), kind=kLoop, calls=%fused_computation.181 | loop fusion | flops 18849792 | bytes 9535488 | tf_op jit(solution)/shard_map/vmap()/reduce_sum | solution.py:44
  138.3 8.0 %fusion.98 = (f32[6144]{0:T(1024)S(1)}, f32[6144]{0:T(1024)S(1)}, f32[6144]{0:T(1024)S(1)}, f32[6144]{0:T(1024)S(1)}, f32[6144]{0:T(1024)S(1)}, /*index=5*/f32[6...) fusion(f32[1,256,6144]{2,1,0:T(8,128)S(1)} %get-tuple-element.45, ...), kind=kLoop, calls=%fused_computation.190 | loop fusion | flops 42412032 | bytes 9658368 | tf_op jit(solution)/shard_map/vmap()/reduce_sum | solution.py:44
  146.5 8.1 %fusion.107 = (f32[6144]{0:T(1024)S(1)}, f32[6144]{0:T(1024)S(1)}, f32[6144]{0:T(1024)S(1)}, f32[6144]{0:T(1024)S(1)}, f32[6144]{0:T(1024)S(1)}, /*index=5*/f32[...) fusion(f32[1,256,6144]{2,1,0:T(8,128)S(1)} %get-tuple-element.45, ...), kind=kLoop, calls=%fused_computation.199 | loop fusion | flops 43978752 | bytes 9682944 | tf_op jit(solution)/shard_map/vmap()/reduce_sum | solution.py:44
  154.6 1.1 stack.127
  155.8 1.1 maximum_bitcast_fusion
  156.8 0.0 reduce-scatter.2.cloned.1.call-update
  156.8 0.0 all-reduce.4.cloned.1.call-start
  156.9 70.8 %reduce-scatter.2.cloned.1.call-done = f32[34,768]{1,0:T(8,128)} async-done(((f32[34,6144]{1,0:T(8,128)}), f32[34,768]{1,0:T(8,128)}) %reduce-scatter.2.cloned.1.call-update) | async-done | bytes 104464 | tf_op jit(solution)/shard_map/reduce_scatter | solution.py:81
  227.7 0.0 all-reduce.4.cloned.1.call-update
  227.9 88.0 %fusion.54 = bf16[1,256,6144]{2,1,0:T(8,128)(2,1)} fusion(f32[1,256,6144]{2,1,0:T(8,128)} %copy-done, f32[6144]{0:T(1024)S(1)} %bitcast.101, f32[6144]{0:T(1024)S(1)} %bitcast.103, f32[6144]{0:T(1024)S(1)} %bitcast.105, f32[6144]{0:T(1024)S(1)} %bitcast.107, f32[6144]{0:T(1024)S(1)} %bitcast.109, f32[6144]{0:T(1024)S(1)} %bitcast.111, ...), kind=kLoop, calls=%fused_computation.146 | loop fusion | flops 97517568 | bytes 10199040 | tf_op jit(solution)/shard_map/vmap()/convert_element_type | solution.py:64
  315.9 0.0 all-reduce.4.cloned.1.call-done
  316.0 0.9 broadcast_multiply_fusion
  316.9 0.6 slice_reduce_fusion
  317.5 0.6 slice.491
  (41 shorter events, 0.1 us)
Async XLA Ops:
  7.2 220.6 %reduce-scatter.2.cloned.1.call-start = ((), (), s32[]{:S(2)}) async-start(), calls=%async_computation.1 | async-start | bytes 1105920 | tf_op jit(solution)/shard_map/reduce_scatter | solution.py:81
  34.9 78.9 %copy-start.3 = (bf16[1,256,6144]{2,1,0:T(8,128)(2,1)S(1)}, bf16[1,256,6144]{2,1,0:T(8,128)(2,1)}, u32[]{:S(2)}) copy-start(bf16[1,256,6144]{2,1,0:T(8,128)(2,1)} %param.7) | copy-start | bytes 9437188
  110.1 4.6 %copy-start.1 = (f32[1,256,6144]{2,1,0:T(8,128)S(1)}, f32[1,256,6144]{2,1,0:T(8,128)}, u32[]{:S(2)}) copy-start(f32[1,256,6144]{2,1,0:T(8,128)} %get-tuple-element.48) | copy-start | bytes 18874372
  114.7 8.9 %copy-start.2 = (bf16[1,256,6144]{2,1,0:T(8,128)(2,1)S(1)}, bf16[1,256,6144]{2,1,0:T(8,128)(2,1)}, u32[]{:S(2)}) copy-start(bf16[1,256,6144]{2,1,0:T(8,128)(2,1)} %param.6) | copy-start | bytes 9437188
  114.7 8.9 %copy-start.19 = (f32[1,6144]{1,0:T(1,128)S(1)}, f32[1,6144]{1,0:T(1,128)}, u32[]{:S(2)}) copy-start(f32[1,6144]{1,0:T(1,128)} %get-tuple-element.50) | copy-start | bytes 73732
  134.7 11.7 %copy-start = (f32[1,256,6144]{2,1,0:T(8,128)}, f32[1,256,6144]{2,1,0:T(8,128)S(1)}, u32[]{:S(2)}) copy-start(f32[1,256,6144]{2,1,0:T(8,128)S(1)} %get-tuple-element.45) | copy-start | bytes 18874372
  146.3 9.4 %copy-start.20 = (f32[6144]{0:T(1024)S(1)}, f32[6144]{0:T(1024)}, u32[]{:S(2)}) copy-start(f32[6144]{0:T(1024)} %get-tuple-element.6) | copy-start | bytes 73732
  146.3 9.4 %copy-start.21 = (f32[6144]{0:T(1024)S(1)}, f32[6144]{0:T(1024)}, u32[]{:S(2)}) copy-start(f32[6144]{0:T(1024)} %get-tuple-element.41) | copy-start | bytes 73732
  146.4 81.4 %copy-start.4 = (f32[1,6144]{1,0:T(1,128)S(1)}, f32[1,6144]{1,0:T(1,128)}, u32[]{:S(2)}) copy-start(f32[1,6144]{1,0:T(1,128)} %get-tuple-element.54) | copy-start | bytes 73732
  146.4 81.4 %copy-start.5 = (f32[1,6144]{1,0:T(1,128)S(1)}, f32[1,6144]{1,0:T(1,128)}, u32[]{:S(2)}) copy-start(f32[1,6144]{1,0:T(1,128)} %get-tuple-element.55) | copy-start | bytes 73732
  146.4 81.4 %copy-start.6 = (f32[1,6144]{1,0:T(1,128)S(1)}, f32[1,6144]{1,0:T(1,128)}, u32[]{:S(2)}) copy-start(f32[1,6144]{1,0:T(1,128)} %get-tuple-element.56) | copy-start | bytes 73732
  146.4 81.4 %copy-start.7 = (f32[1,6144]{1,0:T(1,128)S(1)}, f32[1,6144]{1,0:T(1,128)}, u32[]{:S(2)}) copy-start(f32[1,6144]{1,0:T(1,128)} %get-tuple-element.57) | copy-start | bytes 73732
  146.4 81.4 %copy-start.8 = (f32[1,6144]{1,0:T(1,128)S(1)}, f32[1,6144]{1,0:T(1,128)}, u32[]{:S(2)}) copy-start(f32[1,6144]{1,0:T(1,128)} %get-tuple-element.58) | copy-start | bytes 73732
  146.4 81.4 %copy-start.9 = (f32[1,6144]{1,0:T(1,128)S(1)}, f32[1,6144]{1,0:T(1,128)}, u32[]{:S(2)}) copy-start(f32[1,6144]{1,0:T(1,128)} %get-tuple-element.59) | copy-start | bytes 73732
  146.4 81.4 %copy-start.10 = (f32[1,6144]{1,0:T(1,128)S(1)}, f32[1,6144]{1,0:T(1,128)}, u32[]{:S(2)}) copy-start(f32[1,6144]{1,0:T(1,128)} %get-tuple-element.60) | copy-start | bytes 73732
  146.4 81.4 %copy-start.11 = (f32[1,6144]{1,0:T(1,128)S(1)}, f32[1,6144]{1,0:T(1,128)}, u32[]{:S(2)}) copy-start(f32[1,6144]{1,0:T(1,128)} %get-tuple-element.61) | copy-start | bytes 73732
  146.4 81.4 %copy-start.12 = (f32[1,6144]{1,0:T(1,128)S(1)}, f32[1,6144]{1,0:T(1,128)}, u32[]{:S(2)}) copy-start(f32[1,6144]{1,0:T(1,128)} %get-tuple-element.62) | copy-start | bytes 73732
  146.4 81.4 %copy-start.13 = (f32[1,6144]{1,0:T(1,128)S(1)}, f32[1,6144]{1,0:T(1,128)}, u32[]{:S(2)}) copy-start(f32[1,6144]{1,0:T(1,128)} %get-tuple-element.63) | copy-start | bytes 73732
  146.5 81.4 %copy-start.14 = (f32[1,6144]{1,0:T(1,128)S(1)}, f32[1,6144]{1,0:T(1,128)}, u32[]{:S(2)}) copy-start(f32[1,6144]{1,0:T(1,128)} %get-tuple-element.64) | copy-start | bytes 73732
  146.5 81.4 %copy-start.15 = (f32[1,6144]{1,0:T(1,128)S(1)}, f32[1,6144]{1,0:T(1,128)}, u32[]{:S(2)}) copy-start(f32[1,6144]{1,0:T(1,128)} %get-tuple-element.65) | copy-start | bytes 73732
  146.5 81.4 %copy-start.16 = (f32[1,6144]{1,0:T(1,128)S(1)}, f32[1,6144]{1,0:T(1,128)}, u32[]{:S(2)}) copy-start(f32[1,6144]{1,0:T(1,128)} %get-tuple-element.66) | copy-start | bytes 73732
  146.5 81.4 %copy-start.17 = (f32[1,6144]{1,0:T(1,128)S(1)}, f32[1,6144]{1,0:T(1,128)}, u32[]{:S(2)}) copy-start(f32[1,6144]{1,0:T(1,128)} %get-tuple-element.67) | copy-start | bytes 73732
  146.5 81.4 %copy-start.18 = (f32[1,6144]{1,0:T(1,128)S(1)}, f32[1,6144]{1,0:T(1,128)}, u32[]{:S(2)}) copy-start(f32[1,6144]{1,0:T(1,128)} %get-tuple-element.68) | copy-start | bytes 73732
  156.8 159.1 %all-reduce.4.cloned.1.call-start = ((), (), s32[]{:S(2)}) async-start(), calls=%async_computation.2 | async-start | bytes 245760 | tf_op jit(solution)/shard_map/psum | solution.py:82
Sparse Core Ops, SparseCore 0:
  157.0 70.7 reduce-scatter.1
  230.1 31.3 all-reduce.3
where the time goes:
time: 329 us; the launch traced here: 325 us
  other arithmetic  211 us (64%)
  waiting for transfers between devices  70.9 us (22%)
  blocking collectives  23 us (7%)
  between operations  14.4 us (4%)
  local copies, waits for them, and re-layouts  5.39 us (2%)
    convert_element_type x1, other arithmetic, backward_part(): return (grad_input.astype(jnp.bfloat16), terms)  88 us
    reduce_sum x1, other arithmetic, forward_part(): row_mean = jnp.mean(conv_out, axis=-1, keepdims=True)  75.1 us
    reduce_scatter x1, waiting for transfers between devices, per_device(): lax.psum_scatter(terms, 'shard', scatter_dimension=1, tiled=True)  70.8 us
    reduce_sum x4, other arithmetic, backward_part(): jnp.sum(grad_conv * padded_in[lag_index:lag_index + length].astype(jnp.fl...  30.8 us
    all_gather x1, blocking collectives, per_device(): gathered = lax.all_gather(packed, 'shard', axis=1, tiled=True)  23 us
    reduce_sum x1, other arithmetic, backward_part(): jnp.sum(grad_affine * normed, axis=0)[None]  8.91 us
  transfers between devices with their start and end apart: 2, of which 1 were waited for; matrix products, arithmetic and copies ran while one was open for 27% of the time, Pallas kernels for 0%

commit v1 on v0

v1 whole, which is shorter than its diff:
```python
import math

import jax
import jax.numpy as jnp
from jax import lax
from jax.experimental import pallas as pl
from jax.experimental.pallas import tpu as pltpu
from jax.sharding import PartitionSpec as P

LANES = 128
ROWS = 8
PAD = 16
PARAM_ROWS = 48
TERM_ROWS = 40


def lanes_of(index):
    return pl.ds(pl.multiple_of(index * LANES, LANES), LANES)


def shifted_taps(src, base, coef_ref, coef_row, count):
    def by_phase(phase, totals):
        totals = list(totals)
        coefs = [
            jnp.broadcast_to(coef_ref[pl.ds(coef_row(ROWS * a + phase), 1), :], (ROWS, LANES))
            for a in range(4)
        ]
        for m in range(count + 3):
            value = src[pl.ds(base + ROWS * m + phase + 1, ROWS), :]
            for a in range(4):
                if 0 <= m - a < count:
                    totals[m - a] = totals[m - a] + coefs[a] * value
        return tuple(totals)

    return by_phase


def local_kernel(taps, x_ref, cot_ref, par_ref, act_ref, gin_ref, terms_ref,
                 xp, gp, conv, pf, row_a, row_b, row_c, row_d, acc):
    frames, width = x_ref.shape
    count = frames // ROWS
    tiles = width // LANES
    zeros_tile = jnp.zeros((ROWS, LANES), jnp.float32)

    def rows(i):
        return pl.ds(ROWS * i, ROWS)

    long = frames + 2 * PAD
    held = ROWS + PARAM_ROWS

    def at_long(c, start, size):
        return pl.ds(pl.multiple_of(c * long + start, ROWS), size)

    def at_held(c, start, size):
        return pl.ds(c * held + start, size)

    row_a[...] = jnp.zeros_like(row_a)
    row_c[...] = jnp.zeros_like(row_c)
    row_d[...] = jnp.zeros_like(row_d)

    def forward(c, carry):
        lanes = lanes_of(c)
        pf[at_held(c, 0, ROWS), :] = zeros_tile
        pf[at_held(c, ROWS, PARAM_ROWS), :] = par_ref[:, lanes].astype(jnp.float32)
        for ref in (xp, gp):
            for start in (0, PAD + frames):
                ref[at_long(c, start, PAD), :] = jnp.zeros((PAD, LANES), jnp.float32)
        xp[at_long(c, PAD, frames), :] = x_ref[:, lanes].astype(jnp.float32)
        bias = jnp.broadcast_to(pf[at_held(c, ROWS + taps + 1, 1), :], (ROWS, LANES))
        totals = lax.fori_loop(
            0,
            ROWS,
            shifted_taps(xp, c * long, pf, lambda j: c * held + ROWS + j, count),
            (bias,) * count,
        )
        for i in range(count):
            conv[rows(i), lanes] = totals[i]
            row_a[rows(i), :] += totals[i]
        return carry

    lax.fori_loop(0, tiles, forward, 0)

    def stats(i, carry):
        at = pl.ds(pl.multiple_of(i * ROWS, ROWS), ROWS)
        mean = jnp.sum(row_a[at, :], axis=-1, keepdims=True) * (1.0 / width)
        mean = jnp.broadcast_to(mean, (ROWS, LANES))
        parts = [zeros_tile] * 4
        for c in range(tiles):
            off = conv[at, c * LANES : (c + 1) * LANES] - mean
            parts[c % 4] = parts[c % 4] + off * off
        square = (parts[0] + parts[1]) + (parts[2] + parts[3])
        var = jnp.sum(square, axis=-1, keepdims=True) * (1.0 / width)
        row_a[at, :] = mean
        row_b[at, :] = jnp.broadcast_to(lax.rsqrt(var + 1e-05), (ROWS, LANES))
        return carry

    lax.fori_loop(0, count, stats, 0)

    def pointwise(c, carry):
        lanes = lanes_of(c)
        gain = jnp.broadcast_to(pf[at_held(c, ROWS + taps + 2, 1), :], (ROWS, LANES))
        shift = jnp.broadcast_to(pf[at_held(c, ROWS + taps + 3, 1), :], (ROWS, LANES))
        for_gain = [zeros_tile] * 2
        for_bias = [zeros_tile] * 2
        for pair in range(count // 2):
            two = pl.ds(2 * ROWS * pair, 2 * ROWS)
            upstream = cot_ref[two, lanes].astype(jnp.float32)
            acts = []
            for half in range(2):
                i = 2 * pair + half
                normed = (conv[rows(i), lanes] - row_a[rows(i), :]) * row_b[rows(i), :]
                affine = gain * normed + shift
                squash = 0.5 + 0.5 * jnp.tanh(0.5 * affine)
                acts.append(affine * squash)
                up = upstream[half * ROWS : (half + 1) * ROWS]
                grad_affine = up * squash * (1.0 + affine * (1.0 - squash))
                grad_normed = grad_affine * gain
                conv[rows(i), lanes] = normed
                gp[at_long(c, PAD + ROWS * i, ROWS), :] = grad_normed
                row_c[rows(i), :] += grad_normed
                row_d[rows(i), :] += grad_normed * normed
                for_gain[half] = for_gain[half] + grad_affine * normed
                for_bias[half] = for_bias[half] + grad_affine
            act_ref[two, lanes] = jnp.concatenate(acts, 0).astype(jnp.bfloat16)
        terms_ref[32:33, lanes] = jnp.sum(for_gain[0] + for_gain[1], axis=0, keepdims=True)
        terms_ref[33:34, lanes] = jnp.sum(for_bias[0] + for_bias[1], axis=0, keepdims=True)
        return carry

    lax.fori_loop(0, tiles, pointwise, 0)

    def means(i, carry):
        at = pl.ds(pl.multiple_of(i * ROWS, ROWS), ROWS)
        for ref in (row_c, row_d):
            mean = jnp.sum(ref[at, :], axis=-1, keepdims=True) * (1.0 / width)
            ref[at, :] = jnp.broadcast_to(mean, (ROWS, LANES))
        return carry

    lax.fori_loop(0, count, means, 0)

    def weights(c, carry):
        lanes = lanes_of(c)
        grads = []
        total = [zeros_tile] * 2
        for i in range(count):
            grad = row_b[rows(i), :] * (
                gp[at_long(c, PAD + ROWS * i, ROWS), :] - row_c[rows(i), :] - conv[rows(i), lanes] * row_d[rows(i), :]
            )
            gp[at_long(c, PAD + ROWS * i, ROWS), :] = grad
            total[i % 2] = total[i % 2] + grad
            grads.append(grad)

        def by_phase(phase, carry):
            sums = [[zeros_tile, zeros_tile] for _ in range(4)]
            for m in range(count + 3):
                value = xp[pl.ds(c * long + ROWS * m + phase + 1, ROWS), :]
                for a in range(4):
                    if 0 <= m - a < count:
                        sums[a][m % 2] = sums[a][m % 2] + grads[m - a] * value
            for a in range(4):
                start = pl.multiple_of((ROWS * a + phase) * ROWS, ROWS)
                acc[pl.ds(start, ROWS), :] = sums[a][0] + sums[a][1]
            return carry

        lax.fori_loop(0, ROWS, by_phase, 0)
        acc[taps * ROWS : (taps + 1) * ROWS, :] = total[0] + total[1]
        summed = acc[pl.ds(0, 32, stride=ROWS), :]
        for s in range(1, ROWS):
            summed = summed + acc[pl.ds(s, 32, stride=ROWS), :]
        terms_ref[0:32, lanes] = summed
        return carry

    lax.fori_loop(0, tiles, weights, 0)

    def inputs(c, carry):
        lanes = lanes_of(c)
        totals = lax.fori_loop(
            0,
            ROWS,
            shifted_taps(gp, c * long, pf, lambda j: c * held + ROWS + taps - 1 - j, count),
            (zeros_tile,) * count,
        )
        for i in range(count // 2):
            both = jnp.concatenate([totals[2 * i], totals[2 * i + 1]], 0)
            gin_ref[pl.ds(2 * ROWS * i, 2 * ROWS), lanes] = both.astype(jnp.bfloat16)
        return carry

    lax.fori_loop(0, tiles, inputs, 0)


def local_part(frames_in, upstream, params, taps):
    frames, width = frames_in.shape
    vmem = pl.BlockSpec(memory_space=pltpu.VMEM)
    f32 = jnp.float32
    return pl.pallas_call(
        lambda *refs: local_kernel(taps, *refs),
        out_shape=(
            jax.ShapeDtypeStruct((frames, width), jnp.bfloat16),
            jax.ShapeDtypeStruct((frames, width), jnp.bfloat16),
            jax.ShapeDtypeStruct((TERM_ROWS, width), f32),
        ),
        in_specs=[vmem] * 3,
        out_specs=(vmem,) * 3,
        scratch_shapes=[
            pltpu.VMEM((width // LANES * (frames + 2 * PAD), LANES), f32),
            pltpu.VMEM((width // LANES * (frames + 2 * PAD), LANES), f32),
            pltpu.VMEM((frames, width), f32),
            pltpu.VMEM((width // LANES * (ROWS + PARAM_ROWS), LANES), f32),
            pltpu.VMEM((frames, LANES), f32),
            pltpu.VMEM((frames, LANES), f32),
            pltpu.VMEM((frames, LANES), f32),
            pltpu.VMEM((frames, LANES), f32),
            pltpu.VMEM((32 * ROWS, LANES), f32),
        ],
        compiler_params=pltpu.CompilerParams(vmem_limit_bytes=56 * 1024 * 1024),
    )(frames_in, upstream, params)


def per_device(conv_input, cotangent, kernel, conv_bias, ln_gain, ln_bias):
    taps = kernel.shape[0]
    packed = jnp.concatenate(
        [kernel, jnp.zeros_like(conv_bias)[None], conv_bias[None], ln_gain[None], ln_bias[None]], 0
    )
    packed = jnp.pad(packed, ((0, PARAM_ROWS - packed.shape[0]), (0, 0)))
    gathered = lax.all_gather(packed, "shard", axis=1, tiled=True)
    activated, grad_input, terms = local_part(conv_input[0], cotangent[0], gathered, taps)
    share_sum = lax.psum_scatter(terms, "shard", scatter_dimension=1, tiled=True)
    summed = lax.psum(share_sum, "rep")
    clips = conv_input.shape[0] * lax.axis_size("rep") * lax.axis_size("shard")
    grads = summed * (1.0 / math.sqrt(clips * conv_input.shape[1]))
    return (activated[None], grad_input[None], grads[:taps], grads[taps], grads[taps + 1], grads[taps + 2])


def solution(mesh):
    clips = P(("rep", "shard"), None, None)
    specs = (P(None, "shard"), P("shard"), P("shard"), P("shard"))
    return jax.shard_map(
        per_device, mesh=mesh, in_specs=(clips, clips) + specs, out_specs=(clips, clips) + specs,
        check_vma=False,
    )
```

time: 329 us -> 231 us (0.70)
  other arithmetic: 211 us -> 0.91 us
  Pallas kernels: 0 us -> 79.7 us
  waiting for transfers between devices: 70.9 us -> 104 us
    reduce_sum x8 -> x0, other arithmetic: 120 us -> none  [the longest x1 75.1 us: forward_part(): row_mean = jnp.mean(conv_out, axis=-1, keepdims=True)]
    convert_element_type x3 -> x0, other arithmetic: 89.9 us -> none  [the longest x1 88 us: backward_part(): return (grad_input.astype(jnp.bfloat16), terms)]
    pallas_call x0 -> x1, Pallas kernels: none -> 79.7 us  [local_part(): pl.pallas_call(lambda *refs: local_kernel(taps, *refs), out_shape=(jax.Sh...]
    psum x1, waiting for transfers between devices: 0.02 us -> 33.8 us  [per_device(): summed = lax.psum(share_sum, 'rep')]
  transfers between devices with their start and end apart: 2 -> 2, of which waited for: 1 -> 2; matrix products, arithmetic and copies ran while one was open for 27% -> 0% of each run, Pallas kernels for 0% -> 0%
where the time goes in v1:
time: 231 us; the launch traced here: 229 us
  waiting for transfers between devices  104 us (45%)
  Pallas kernels  79.7 us (35%)
  blocking collectives  25.4 us (11%)
  between operations  14 us (6%)
  local copies, waits for them, and re-layouts  4.2 us (2%)
    pallas_call x1, Pallas kernels, local_part(): pl.pallas_call(lambda *refs: local_kernel(taps, *refs), out_shape=(jax.Sh...  79.7 us
    reduce_scatter x1, waiting for transfers between devices, per_device(): lax.psum_scatter(terms, 'shard', scatter_dimension=1, tiled=True)  70.6 us
    psum x1, waiting for transfers between devices, per_device(): summed = lax.psum(share_sum, 'rep')  33.8 us
    all_gather x1, blocking collectives, per_device(): gathered = lax.all_gather(packed, 'shard', axis=1, tiled=True)  25.4 us
  transfers between devices with their start and end apart: 2, of which 2 were waited for; matrix products, arithmetic and copies ran while one was open for 0% of the time, Pallas kernels for 0%

profile of v1, /device:TPU:13, one launch (start us, length us, event | category | flops | bytes accessed | tf_op | source)
XLA Modules:
  0.0 228.8 jit_solution(311315411345895410)
XLA Ops:
  7.2 0.0 reduce-scatter.2.cloned.1.call-start
  7.2 0.7 broadcast_in_dim.15
  7.9 0.7 broadcast_in_dim.16
  8.6 0.7 broadcast_in_dim.17
  9.3 0.9 concatenate.3
  10.1 25.4 %all_gather.3.refs_2_ = bf16[48,6144]{1,0:T(8,128)(2,1)} all-gather(bf16[48,768]{1,0:T(8,128)(2,1)S(1)} %pad.4), channel_id=1, replica_groups=mesh['rep'=4,'shard'=8] {'shard'}, dimensions={1}, use_global_device_ids=true | all-gather | bytes 663552 | tf_op jit(solution)/shard_map/all_gather | solution.py:224
  35.6 79.7 %shard_map.109 = (bf16[256,6144]{1,0:T(8,128)(2,1)}, bf16[256,6144]{1,0:T(8,128)(2,1)}, f32[40,6144]{1,0:T(8,128)}) custom-call(bf16[256,6144]{1,0:T(8,128)(2,1)} %bitcast.4, bf16[256,6144]{1,0:T(8,128)(2,1)} %bitcast.5, bf16[48,6144]{1,0:T(8,128)(2,1)} %all_gather.3.refs_2_), custom_call_target="tpu_custom_call" | custom-call | tf_op jit(solution)/shard_map/pallas_call | solution.py:194
  115.2 0.0 reduce-scatter.2.cloned.1.call-update
  115.3 0.0 all-reduce.3.cloned.1.call-start
  115.3 70.6 %reduce-scatter.2.cloned.1.call-done = f32[40,768]{1,0:T(8,128)} async-done(((f32[40,6144]{1,0:T(8,128)}), f32[40,768]{1,0:T(8,128)}) %reduce-scatter.2.cloned.1.call-update) | async-done | bytes 122896 | tf_op jit(solution)/shard_map/reduce_scatter | solution.py:226
  185.9 0.0 all-reduce.3.cloned.1.call-update
  186.0 33.8 %all-reduce.3.cloned.1.call-done = f32[40,768]{1,0:T(8,128)} async-done(((f32[40,768]{1,0:T(8,128)}), f32[40,768]{1,0:T(8,128)}) %all-reduce.3.cloned.1.call-update) | async-done | bytes 122896 | tf_op jit(solution)/shard_map/psum | solution.py:227
  219.8 0.9 broadcast_multiply_fusion
  220.7 0.6 slice_reduce_fusion
  221.3 0.6 slice.16
  (2 shorter events, 0.0 us)
Async XLA Ops:
  7.2 178.8 %reduce-scatter.2.cloned.1.call-start = ((), (), s32[]{:S(2)}) async-start(), calls=%async_computation.1 | async-start | bytes 1105920 | tf_op jit(solution)/shard_map/reduce_scatter | solution.py:226
  115.3 104.5 %all-reduce.3.cloned.1.call-start = ((), (), s32[]{:S(2)}) async-start(), calls=%async_computation.2 | async-start | bytes 245760 | tf_op jit(solution)/shard_map/psum | solution.py:227
Sparse Core Ops, SparseCore 0:
  115.4 70.5 reduce-scatter.1
  188.4 31.3 all-reduce.2

commit v2 on v1

--- a/solution.py
+++ b/solution.py
@@ -40,6 +40,7 @@
     frames, width = x_ref.shape
     count = frames // ROWS
     tiles = width // LANES
+    per = tiles // par_ref.shape[0]
     zeros_tile = jnp.zeros((ROWS, LANES), jnp.float32)
 
     def rows(i):
@@ -61,7 +62,7 @@
     def forward(c, carry):
         lanes = lanes_of(c)
         pf[at_held(c, 0, ROWS), :] = zeros_tile
-        pf[at_held(c, ROWS, PARAM_ROWS), :] = par_ref[:, lanes].astype(jnp.float32)
+        pf[at_held(c, ROWS, PARAM_ROWS), :] = par_ref[c // per, :, lanes_of(c % per)].astype(jnp.float32)
         for ref in (xp, gp):
             for start in (0, PAD + frames):
                 ref[at_long(c, start, PAD), :] = jnp.zeros((PAD, LANES), jnp.float32)
@@ -122,8 +123,9 @@
                 for_gain[half] = for_gain[half] + grad_affine * normed
                 for_bias[half] = for_bias[half] + grad_affine
             act_ref[two, lanes] = jnp.concatenate(acts, 0).astype(jnp.bfloat16)
-        terms_ref[32:33, lanes] = jnp.sum(for_gain[0] + for_gain[1], axis=0, keepdims=True)
-        terms_ref[33:34, lanes] = jnp.sum(for_bias[0] + for_bias[1], axis=0, keepdims=True)
+        terms_ref[c // per, 32:40, lanes_of(c % per)] = zeros_tile
+        terms_ref[c // per, 32:33, lanes_of(c % per)] = jnp.sum(for_gain[0] + for_gain[1], axis=0, keepdims=True)
+        terms_ref[c // per, 33:34, lanes_of(c % per)] = jnp.sum(for_bias[0] + for_bias[1], axis=0, keepdims=True)
         return carry
 
     lax.fori_loop(0, tiles, pointwise, 0)
@@ -166,7 +168,7 @@
         summed = acc[pl.ds(0, 32, stride=ROWS), :]
         for s in range(1, ROWS):
             summed = summed + acc[pl.ds(s, 32, stride=ROWS), :]
-        terms_ref[0:32, lanes] = summed
+        terms_ref[c // per, 0:32, lanes_of(c % per)] = summed
         return carry
 
     lax.fori_loop(0, tiles, weights, 0)
@@ -196,7 +198,7 @@
         out_shape=(
             jax.ShapeDtypeStruct((frames, width), jnp.bfloat16),
             jax.ShapeDtypeStruct((frames, width), jnp.bfloat16),
-            jax.ShapeDtypeStruct((TERM_ROWS, width), f32),
+            jax.ShapeDtypeStruct((params.shape[0], TERM_ROWS, params.shape[2]), f32),
         ),
         in_specs=[vmem] * 3,
         out_specs=(vmem,) * 3,
@@ -215,18 +217,126 @@
     )(frames_in, upstream, params)
 
 
+def greet(axis_sizes):
+    barrier = pltpu.get_barrier_semaphore()
+    for axis, size in axis_sizes:
+        for k in range(1, size):
+            peer = lax.rem(lax.axis_index(axis) + k, size)
+            pl.semaphore_signal(
+                barrier, inc=1, device_id={axis: peer}, device_id_type=pl.DeviceIdType.MESH
+            )
+    pl.semaphore_wait(barrier, sum(size - 1 for _, size in axis_sizes))
+
+
+def send(src, dst, sems, k, axis, peer):
+    copy = pltpu.make_async_remote_copy(
+        src_ref=src,
+        dst_ref=dst,
+        send_sem=sems[0].at[k - 1],
+        recv_sem=sems[1].at[k - 1],
+        device_id={axis: peer},
+        device_id_type=pl.DeviceIdType.MESH,
+    )
+    copy.start()
+    return copy
+
+
+def gather_kernel(groups, own_ref, out_ref, held, send_sem, recv_sem):
+    me = lax.axis_index("shard")
+    greet([("shard", groups)])
+    copies = [
+        send(own_ref, held.at[k - 1], (send_sem, recv_sem), k, "shard", lax.rem(me + k, groups))
+        for k in range(1, groups)
+    ]
+    out_ref[me] = own_ref[...]
+    for k in range(1, groups):
+        copies[k - 1].wait()
+        out_ref[lax.rem(me + groups - k, groups)] = held[k - 1]
+
+
+def sum_kernel(groups, replicas, factor, terms_ref, out_ref, held, part, sems_a, sems_b, sems_c, sems_d):
+    me = lax.axis_index("shard")
+    mine = lax.axis_index("rep")
+    greet([("shard", groups), ("rep", replicas)])
+    copies = []
+    for k in range(1, groups):
+        peer = lax.rem(me + k, groups)
+        copies.append(send(terms_ref.at[peer], held.at[k - 1], (sems_a, sems_b), k, "shard", peer))
+    total = terms_ref[me]
+    for k in range(1, groups):
+        copies[k - 1].wait()
+        total = total + held[k - 1]
+    part[mine] = total
+    copies = [
+        send(part.at[mine], part.at[mine], (sems_c, sems_d), k, "rep", lax.rem(mine + k, replicas))
+        for k in range(1, replicas)
+    ]
+    for copy in copies:
+        copy.wait()
+    total = part[0]
+    for r in range(1, replicas):
+        total = total + part[r]
+    out_ref[...] = total * factor
+
+
+def gather(packed, groups):
+    vmem = pl.BlockSpec(memory_space=pltpu.VMEM)
+    sems = pltpu.SemaphoreType.DMA((groups - 1,))
+    return pl.pallas_call(
+        lambda *refs: gather_kernel(groups, *refs),
+        out_shape=jax.ShapeDtypeStruct((groups,) + packed.shape, packed.dtype),
+        in_specs=[vmem],
+        out_specs=vmem,
+        scratch_shapes=[pltpu.VMEM((groups - 1,) + packed.shape, packed.dtype), sems, sems],
+        compiler_params=pltpu.CompilerParams(
+            collective_id=0, has_side_effects=True, vmem_limit_bytes=16 * 1024 * 1024
+        ),
+    )(packed)
+
+
+def sum_terms(terms, groups, replicas, factor):
+    vmem = pl.BlockSpec(memory_space=pltpu.VMEM)
+    block = terms.shape[1:]
+    dma = pltpu.SemaphoreType.DMA
+    return pl.pallas_call(
+        lambda *refs: sum_kernel(groups, replicas, factor, *refs),
+        out_shape=jax.ShapeDtypeStruct(block, jnp.float32),
+        in_specs=[vmem],
+        out_specs=vmem,
+        scratch_shapes=[
+            pltpu.VMEM((groups - 1,) + block, jnp.float32),
+            pltpu.VMEM((replicas,) + block, jnp.float32),
+            dma((groups - 1,)),
+            dma((groups - 1,)),
+            dma((replicas - 1,)),
+            dma((replicas - 1,)),
+        ],
+        compiler_params=pltpu.CompilerParams(
+            collective_id=1, has_side_effects=True, vmem_limit_bytes=16 * 1024 * 1024
+        ),
+    )(terms)
+
+
 def per_device(conv_input, cotangent, kernel, conv_bias, ln_gain, ln_bias):
-    taps = kernel.shape[0]
+    taps, chunk = kernel.shape
+    groups, replicas = lax.axis_size("shard"), lax.axis_size("rep")
+    clips = conv_input.shape[0] * replicas * groups
+    factor = 1.0 / math.sqrt(clips * conv_input.shape[1])
     packed = jnp.concatenate(
         [kernel, jnp.zeros_like(conv_bias)[None], conv_bias[None], ln_gain[None], ln_bias[None]], 0
     )
     packed = jnp.pad(packed, ((0, PARAM_ROWS - packed.shape[0]), (0, 0)))
-    gathered = lax.all_gather(packed, "shard", axis=1, tiled=True)
+    direct = chunk % LANES == 0
+    if direct:
+        gathered = gather(packed, groups)
+    else:
+        gathered = lax.all_gather(packed, "shard", axis=1, tiled=True)[None]
     activated, grad_input, terms = local_part(conv_input[0], cotangent[0], gathered, taps)
-    share_sum = lax.psum_scatter(terms, "shard", scatter_dimension=1, tiled=True)
-    summed = lax.psum(share_sum, "rep")
-    clips = conv_input.shape[0] * lax.axis_size("rep") * lax.axis_size("shard")
-    grads = summed * (1.0 / math.sqrt(clips * conv_input.shape[1]))
+    if direct:
+        grads = sum_terms(terms, groups, replicas, factor)
+    else:
+        share_sum = lax.psum_scatter(terms[0], "shard", scatter_dimension=1, tiled=True)
+        grads = lax.psum(share_sum, "rep") * factor
     return (activated[None], grad_input[None], grads[:taps], grads[taps], grads[taps + 1], grads[taps + 2])
 
 

time: 231 us -> 136 us (0.59)
  waiting for transfers between devices: 104 us -> 0 us
  Pallas kernels: 79.7 us -> 128 us
  blocking collectives: 25.4 us -> 0 us
  between operations: 14 us -> 0.66 us
    reduce_scatter x1 -> x0, waiting for transfers between devices: 70.6 us -> none  [per_device(): lax.psum_scatter(terms, 'shard', scatter_dimension=1, tiled=True)]
    pallas_call x0 -> x2, Pallas kernels: none -> 48.8 us  [the longest x1 31.3 us: sum_terms(): pl.pallas_call(lambda *refs: sum_kernel(groups, replicas, factor, *refs),...]
    psum x1 -> x0, waiting for transfers between devices: 33.8 us -> none  [per_device(): summed = lax.psum(share_sum, 'rep')]
    all_gather x1 -> x0, blocking collectives: 25.4 us -> none  [per_device(): gathered = lax.all_gather(packed, 'shard', axis=1, tiled=True)]
  transfers between devices with their start and end apart: 2 -> 0, of which waited for: 2 -> 0; matrix products, arithmetic and copies ran while one was open for 0% -> 0% of each run, Pallas kernels for 0% -> 0%
where the time goes in v2:
time: 136 us; the launch traced here: 135 us
  Pallas kernels  128 us (94%)
  local copies, waits for them, and re-layouts  6.23 us (5%)
    pallas_call x1, Pallas kernels, local_part(): pl.pallas_call(lambda *refs: local_kernel(taps, *refs), out_shape=(jax.Sh...  79.6 us
    pallas_call x1, Pallas kernels, sum_terms(): pl.pallas_call(lambda *refs: sum_kernel(groups, replicas, factor, *refs),...  31.3 us
    pallas_call x1, Pallas kernels, gather(): pl.pallas_call(lambda *refs: gather_kernel(groups, *refs), out_shape=jax....  17.5 us

profile of v2, /device:TPU:13, one launch (start us, length us, event | category | flops | bytes accessed | tf_op | source)
XLA Modules:
  0.0 135.3 jit_solution(4989929984177489947)
XLA Ops:
  0.6 0.7 broadcast_in_dim.15
  1.3 0.7 broadcast_in_dim.16
  2.0 0.7 broadcast_in_dim.17
  2.7 0.9 concatenate.3
  3.6 17.5 %shard_map.109.refs_2_ = bf16[8,48,768]{2,1,0:T(8,128)(2,1)S(1)} custom-call(bf16[48,768]{1,0:T(8,128)(2,1)S(1)} %pad.4.refs_0_), custom_call_target="tpu_custom_call" | custom-call | tf_op jit(solution)/shard_map/pallas_call | solution.py:285
  21.1 0.0 copy-start
  21.1 0.8 copy-done
  21.9 79.6 %shard_map.110 = (bf16[256,6144]{1,0:T(8,128)(2,1)}, bf16[256,6144]{1,0:T(8,128)(2,1)}, f32[8,40,768]{2,1,0:T(8,128)}) custom-call(bf16[256,6144]{1,0:T(8,128)(2,1)} %bitcast.4, bf16[256,6144]{1,0:T(8,128)(2,1)} %bitcast.5, bf16[8,48,768]{2,1,0:T(8,128)(2,1)} %copy-done), custom_call_target="tpu_custom_call" | custom-call | tf_op jit(solution)/shard_map/pallas_call | solution.py:196
  101.5 0.0 copy-start.1
  101.5 1.2 copy-done.1
  102.7 31.3 %shard_map.111 = f32[40,768]{1,0:T(8,128)S(1)} custom-call(f32[8,40,768]{2,1,0:T(8,128)S(1)} %copy-done.1), custom_call_target="tpu_custom_call" | custom-call | tf_op jit(solution)/shard_map/pallas_call | solution.py:301
  134.0 0.6 slice_reduce_fusion
  134.6 0.6 slice.12
  (2 shorter events, 0.0 us)
Async XLA Ops:
  21.1 0.8 copy-start
  101.5 1.2 copy-start.1

commit v3 on v2

--- a/solution.py
+++ b/solution.py
@@ -73,6 +73,7 @@
             ROWS,
             shifted_taps(xp, c * long, pf, lambda j: c * held + ROWS + j, count),
             (bias,) * count,
+            unroll=True,
         )
         for i in range(count):
             conv[rows(i), lanes] = totals[i]
@@ -163,7 +164,7 @@
                 acc[pl.ds(start, ROWS), :] = sums[a][0] + sums[a][1]
             return carry
 
-        lax.fori_loop(0, ROWS, by_phase, 0)
+        lax.fori_loop(0, ROWS, by_phase, 0, unroll=True)
         acc[taps * ROWS : (taps + 1) * ROWS, :] = total[0] + total[1]
         summed = acc[pl.ds(0, 32, stride=ROWS), :]
         for s in range(1, ROWS):
@@ -180,6 +181,7 @@
             ROWS,
             shifted_taps(gp, c * long, pf, lambda j: c * held + ROWS + taps - 1 - j, count),
             (zeros_tile,) * count,
+            unroll=True,
         )
         for i in range(count // 2):
             both = jnp.concatenate([totals[2 * i], totals[2 * i + 1]], 0)

time: 136 us -> 121 us (0.89)
  Pallas kernels: 128 us -> 114 us
    pallas_call x1, Pallas kernels: 79.6 us -> 65.2 us  [local_part(): pl.pallas_call(lambda *refs: local_kernel(taps, *refs), out_shape=(jax.Sh...]
where the time goes in v3:
time: 121 us
  Pallas kernels  114 us (94%)
  local copies, waits for them, and re-layouts  6.23 us (5%)
    pallas_call x1, Pallas kernels, local_part(): pl.pallas_call(lambda *refs: local_kernel(taps, *refs), out_shape=(jax.Sh...  65.2 us
    pallas_call x1, Pallas kernels, sum_terms(): pl.pallas_call(lambda *refs: sum_kernel(groups, replicas, factor, *refs),...  31.3 us
    pallas_call x1, Pallas kernels, gather(): pl.pallas_call(lambda *refs: gather_kernel(groups, *refs), out_shape=jax....  17.5 us

profile of v3, /device:TPU:13, one launch (start us, length us, event | category | flops | bytes accessed | tf_op | source)
XLA Modules:
  0.0 120.9 jit_solution(7725786747943040237)
XLA Ops:
  0.6 0.7 broadcast_in_dim.15
  1.3 0.7 broadcast_in_dim.16
  2.0 0.7 broadcast_in_dim.17
  2.7 0.9 concatenate.3
  3.6 17.5 %shard_map.109.refs_2_ = bf16[8,48,768]{2,1,0:T(8,128)(2,1)S(1)} custom-call(bf16[48,768]{1,0:T(8,128)(2,1)S(1)} %pad.4.refs_0_), custom_call_target="tpu_custom_call" | custom-call | tf_op jit(solution)/shard_map/pallas_call | solution.py:287
  21.1 0.0 copy-start
  21.1 0.8 copy-done
  21.9 65.2 %shard_map.110 = (bf16[256,6144]{1,0:T(8,128)(2,1)}, bf16[256,6144]{1,0:T(8,128)(2,1)}, f32[8,40,768]{2,1,0:T(8,128)}) custom-call(bf16[256,6144]{1,0:T(8,128)(2,1)} %bitcast.4, bf16[256,6144]{1,0:T(8,128)(2,1)} %bitcast.5, bf16[8,48,768]{2,1,0:T(8,128)(2,1)} %copy-done), custom_call_target="tpu_custom_call" | custom-call | tf_op jit(solution)/shard_map/pallas_call | solution.py:198
  87.1 0.0 copy-start.1
  87.1 1.2 copy-done.1
  88.3 31.3 %shard_map.111 = f32[40,768]{1,0:T(8,128)S(1)} custom-call(f32[8,40,768]{2,1,0:T(8,128)S(1)} %copy-done.1), custom_call_target="tpu_custom_call" | custom-call | tf_op jit(solution)/shard_map/pallas_call | solution.py:303
  119.6 0.6 slice_reduce_fusion
  120.3 0.6 slice.12
  (2 shorter events, 0.0 us)
Async XLA Ops:
  21.1 0.8 copy-start
  87.1 1.2 copy-start.1

commit v4 on v3

--- a/solution.py
+++ b/solution.py
@@ -96,7 +96,7 @@
         row_b[at, :] = jnp.broadcast_to(lax.rsqrt(var + 1e-05), (ROWS, LANES))
         return carry
 
-    lax.fori_loop(0, count, stats, 0)
+    lax.fori_loop(0, count, stats, 0, unroll=4)
 
     def pointwise(c, carry):
         lanes = lanes_of(c)
@@ -138,7 +138,7 @@
             ref[at, :] = jnp.broadcast_to(mean, (ROWS, LANES))
         return carry
 
-    lax.fori_loop(0, count, means, 0)
+    lax.fori_loop(0, count, means, 0, unroll=8)
 
     def weights(c, carry):
         lanes = lanes_of(c)

time: 121 us -> 115 us (0.950)
  Pallas kernels: 114 us -> 108 us
    pallas_call x1, Pallas kernels: 65.2 us -> 59.2 us  [local_part(): pl.pallas_call(lambda *refs: local_kernel(taps, *refs), out_shape=(jax.Sh...]
where the time goes in v4:
time: 115 us
  Pallas kernels  108 us (94%)
  local copies, waits for them, and re-layouts  6.23 us (5%)
    pallas_call x1, Pallas kernels, local_part(): pl.pallas_call(lambda *refs: local_kernel(taps, *refs), out_shape=(jax.Sh...  59.2 us
    pallas_call x1, Pallas kernels, sum_terms(): pl.pallas_call(lambda *refs: sum_kernel(groups, replicas, factor, *refs),...  31.3 us
    pallas_call x1, Pallas kernels, gather(): pl.pallas_call(lambda *refs: gather_kernel(groups, *refs), out_shape=jax....  17.5 us

profile of v4, /device:TPU:13, one launch (start us, length us, event | category | flops | bytes accessed | tf_op | source)
XLA Modules:
  0.0 114.9 jit_solution(13921537435365570274)
XLA Ops:
  0.6 0.7 broadcast_in_dim.15
  1.3 0.7 broadcast_in_dim.16
  2.0 0.7 broadcast_in_dim.17
  2.7 0.9 concatenate.3
  3.6 17.5 %shard_map.109.refs_2_ = bf16[8,48,768]{2,1,0:T(8,128)(2,1)S(1)} custom-call(bf16[48,768]{1,0:T(8,128)(2,1)S(1)} %pad.4.refs_0_), custom_call_target="tpu_custom_call" | custom-call | tf_op jit(solution)/shard_map/pallas_call | solution.py:287
  21.1 0.0 copy-start
  21.1 0.8 copy-done
  21.9 59.2 %shard_map.110 = (bf16[256,6144]{1,0:T(8,128)(2,1)}, bf16[256,6144]{1,0:T(8,128)(2,1)}, f32[8,40,768]{2,1,0:T(8,128)}) custom-call(bf16[256,6144]{1,0:T(8,128)(2,1)} %bitcast.4, bf16[256,6144]{1,0:T(8,128)(2,1)} %bitcast.5, bf16[8,48,768]{2,1,0:T(8,128)(2,1)} %copy-done), custom_call_target="tpu_custom_call" | custom-call | tf_op jit(solution)/shard_map/pallas_call | solution.py:198
  81.1 0.0 copy-start.1
  81.1 1.2 %copy-done.1 = f32[8,40,768]{2,1,0:T(8,128)S(1)} copy-done((f32[8,40,768]{2,1,0:T(8,128)S(1)}, f32[8,40,768]{2,1,0:T(8,128)}, u32[]{:S(2)}) %copy-start.1) | copy-done | bytes 983064
  82.3 31.3 %shard_map.111 = f32[40,768]{1,0:T(8,128)S(1)} custom-call(f32[8,40,768]{2,1,0:T(8,128)S(1)} %copy-done.1), custom_call_target="tpu_custom_call" | custom-call | tf_op jit(solution)/shard_map/pallas_call | solution.py:303
  113.6 0.6 slice_reduce_fusion
  114.2 0.6 slice.12
  (2 shorter events, 0.0 us)
Async XLA Ops:
  21.1 0.8 copy-start
  81.1 1.2 %copy-start.1 = (f32[8,40,768]{2,1,0:T(8,128)S(1)}, f32[8,40,768]{2,1,0:T(8,128)}, u32[]{:S(2)}) copy-start(f32[8,40,768]{2,1,0:T(8,128)} %get-tuple-element.11.refs_0_) | copy-start | bytes 2949124
